TPU v7x, 32 devices: a whole 2x2x4 slice. The times are simulated.
32 devices in a mesh: node: 8 (over y, x, core), state: 4 (over z).
Axes of the slice: x: 2, y: 2, z: 4, core: 2. Of those that a mesh axis runs over, the one named last changes fastest.
Arguments:
- states: float32 [6144, 3072], P('node', 'state'), may hold values from -0.078125 to 0.078125
- coeffs: float32 [3072, 512], P('state'), may hold values from -6 to 6
- cell_matrix: float32 [96, 125, 125], P('node'), may hold values from -0.5 to 0.5
- connect: int32 [96, 125], P('node'), may hold values from 0 to 831, as said below
- face_list: int32 [512], P('node'), may hold values from 0 to 767, as said below
- node_mass: float32 [6144], P('node'), may hold values from 0.25 to 4
Outputs:
- rotated: float32 [512, 6144], P('state', 'node')
- h_panel: float32 [512, 3072], P('node', 'state')
- m_panel: float32 [512, 3072], P('node', 'state')
Inputs may be any that keep to these rules, and one draw needn't show every extreme that they name: `connect`: within each partition the cells cover a periodic in-plane slab of hexahedral elements of order 4; indices 768 and above name ghosts, every ghost and every owned node is used by some cell. `face_list`: the 64 entries of one partition are distinct.
All inputs are finite; a program needn't handle non-finite values.
Results may differ from a plain program's by a relative error of at most 0.000084.
Values sent between devices are 32-bit elements; how exact they have to be, the bound alone decides.
A program may use at most 64 MiB of HBM per device.

v0:
```python
import jax
import jax.numpy as jnp
from jax import lax
from jax.sharding import PartitionSpec as P


def shifted(shard, axis, by):
    length = lax.axis_size(axis)
    pairs = [(i, i + by) for i in range(length) if 0 <= i + by < length]
    return lax.ppermute(shard, axis, pairs)


def apply_cells(block_rows, cell_matrix, connect, face_list):
    height = block_rows.shape[0]
    owned_count = block_rows.shape[1]
    face_values = block_rows[:, face_list]
    ghosts = shifted(face_values, "node", -1)
    extended = jnp.concatenate([block_rows, ghosts], axis=1)
    cell_values = extended[:, connect]
    symmetric = 0.5 * (cell_matrix + jnp.swapaxes(cell_matrix, 1, 2))
    cell_output = jnp.einsum(
        "cab,rcb->rca", symmetric, cell_values, precision=lax.Precision.HIGHEST
    )
    assembled = (
        jnp.zeros(extended.shape, jnp.float32)
        .at[:, connect.reshape(-1)]
        .add(cell_output.reshape(height, -1))
    )
    returned = shifted(assembled[:, owned_count:], "node", 1)
    return assembled[:, :owned_count].at[:, face_list].add(returned)


def local(states, coeffs, cell_matrix, connect, face_list, node_mass):
    state_width = states.shape[1]
    rotated = lax.psum_scatter(
        lax.dot_general(
            coeffs,
            states,
            (((0,), (1,)), ((), ())),
            precision=lax.Precision.HIGHEST,
            preferred_element_type=jnp.float32,
        ),
        "state",
        scatter_dimension=0,
        tiled=True,
    )
    applied = apply_cells(rotated, cell_matrix, connect, face_list)
    stacked = jnp.stack([applied, rotated * node_mass[None, :]], 0)
    pieces = lax.all_gather(stacked, "state", axis=1, tiled=True)
    hamilton = jnp.dot(
        pieces[0], states, precision=lax.Precision.HIGHEST, preferred_element_type=jnp.float32
    )
    correlation = jnp.dot(
        pieces[1], states, precision=lax.Precision.HIGHEST, preferred_element_type=jnp.float32
    )
    partial_value = jnp.concatenate([hamilton, correlation], axis=1)
    own_rows = lax.psum_scatter(partial_value, "node", scatter_dimension=0, tiled=True)
    return (rotated, own_rows[:, :state_width], own_rows[:, state_width:])


def solution(mesh):
    return jax.shard_map(
        local,
        mesh=mesh,
        in_specs=(
            P("node", "state"),
            P("state", None),
            P("node", None, None),
            P("node", None),
            P("node"),
            P("node"),
        ),
        out_specs=(P("state", "node"), P("node", "state"), P("node", "state")),
        check_vma=False,
    )
```

profile of v0, /device:TPU:0, one launch (start us, length us, event | category | flops | bytes accessed | tf_op | source)
XLA Modules:
  0.0 224.5 jit_solution(14853132492181482445)
XLA Ops:
  7.2 0.0 copy-start
  7.2 0.0 copy-start.5
  7.2 0.0 copy-start.8
  7.2 0.0 reduce-scatter.3.cloned.1.call-start
  7.2 1.6 copy-done
  8.8 10.0 %fusion.14 = f32[512,768]{1,0:T(8,128)} fusion(f32[768,512]{1,0:T(8,128)} %param.7, f32[768,768]{1,0:T(8,128)S(1)} %copy-done), kind=kOutput, calls=%fused_computation.30 | convolution fusion | flops 3623878656 | bytes 5505024 | tf_op jit(solution)/shard_map/dot_general | solution.py:36
  18.9 0.0 copy-start.3
  18.9 0.0 reduce-scatter.3.cloned.1.call-update
  18.9 0.0 all-gather.2.cloned.1.call-start
  18.9 0.0 copy-done.5
  19.0 0.1 reshape.41
  19.1 0.1 reshape.53
  19.1 0.0 copy-done.8
  19.2 0.0 copy-start.7
  19.2 0.6 fusion.11
  19.8 0.0 copy-done.7
  19.8 37.2 %reduce-scatter.3.cloned.1.call-done = f32[128,768]{1,0:T(8,128)} async-done(((f32[512,768]{1,0:T(8,128)}), f32[128,768]{1,0:T(8,128)}) %reduce-scatter.3.cloned.1.call-update) | async-done | bytes 393232 | tf_op jit(solution)/shard_map/reduce_scatter | solution.py:35
  57.1 0.0 copy-start.1
  57.1 2.0 copy.9
  59.0 2.2 gather_fusion
  61.2 1.5 copy.10
  62.7 1.5 collective-permute-start
  64.2 0.6 pad_clamp_fusion
  64.8 0.0 copy-done.3
  64.8 1.2 copy.13
  66.0 0.2 collective-permute-done
  66.2 0.0 copy-done.1
  66.2 0.9 pad_maximum_fusion.2
  67.1 0.2 copy.11
  67.3 3.2 %gather_fusion.1 = f32[1500,128]{1,0:T(8,128)S(1)} fusion(f32[128,832]{0,1:T(8,128)S(1)} %copy.11, s32[2048]{0:T(1024)} %pad_clamp_fusion), kind=kCustom, calls=%fused_computation.1 | custom fusion | bytes 1542000 | tf_op jit(solution)/shard_map/gather | solution.py:19
  70.4 0.9 reshape.56
  71.4 1.4 copy.12
  72.8 0.0 copy-start.2
  72.8 0.0 copy-start.6
  72.8 4.0 %convolution_bitcast_fusion = f32[128,12,125]{0,2,1:T(8,128)} fusion(f32[12,125,125]{2,1,0:T(8,128)} %param.8, f32[12,125,125]{1,2,0:T(8,128)} %copy.13, f32[12,125,128]{1,2,0:T(8,128)S(1)} %copy.12), kind=kOutput, calls=%fused_computation.9 | convolution fusion | flops 288375008 | bytes 3036000 | tf_op jit(solution)/shard_map/cab,rcb->rca/dot_general | solution.py:21
  76.9 1.2 reshape.60
  78.0 8.9 %scatter_custom_fusion = f32[128,832]{0,1:T(8,128)} fusion(s32[1500]{0:T(1024)} %fusion.11, f32[128,1500]{0,1:T(8,128)S(1)} %reshape.60, f32[]{:T(128)} %constant.5.clone.1), kind=kCustom, calls=%fused_computation.14 | custom fusion | flops 192000 | bytes 1194496 | tf_op jit(solution)/shard_map/scatter-add | solution.py:27
  86.9 0.8 slice.29
  87.7 4.1 %collective-permute-start.1 = (f32[128,64]{0,1:T(8,128)S(1)}, f32[128,64]{0,1:T(8,128)S(1)}, u32[]{:S(2)}, u32[]{:S(2)}) collective-permute-start(f32[128,64]{0,1:T(8,128)S(1)} %slice.29), channel_id=1, source_target_pairs={{0,4},{4,8},{8,12},{12,16},{16,20},{20,24},{24,28},{1,5},{5,9},{9,... | collective-permute-start | bytes 98312 | tf_op jit(solution)/shard_map/ppermute | solution.py:10
  91.8 0.0 copy-done.2
  91.8 0.0 copy-done.6
  91.9 1.0 slice.28
  92.9 0.0 collective-permute-done.1
  92.9 1.2 scatter_custom_fusion.1
  94.1 0.2 copy.14
  94.3 0.9 pad_maximum_fusion.1
  95.2 0.0 all-gather.2.cloned.1.call-update
  95.2 0.3 reduce-scatter.5.cloned.1.call-start
  95.5 63.9 %all-gather.2.cloned.1.call-done = f32[2,512,768]{2,1,0:T(8,128)} async-done(((f32[2,128,768]{2,1,0:T(8,128)}), f32[2,512,768]{2,1,0:T(8,128)}) %all-gather.2.cloned.1.call-update) | async-done | bytes 3145744 | tf_op jit(solution)/shard_map/all_gather | solution.py:49
  159.4 0.0 copy-start.4
  159.4 5.6 %fusion = f32[512,768]{1,0:T(8,128)S(1)} fusion(f32[768,768]{1,0:T(8,128)S(1)} %copy-done, f32[2,512,768]{2,1,0:T(8,128)} %all-gather.2.cloned.1.call-done), kind=kOutput, calls=%fused_computation.6 | convolution fusion | flops 3623878656 | bytes 5505024 | tf_op jit(solution)/shard_map/dot_general | solution.py:53
  165.0 0.0 copy-done.4
  165.0 4.0 %fusion.1 = f32[512,768]{1,0:T(8,128)S(1)} fusion(f32[768,768]{1,0:T(8,128)S(1)} %copy-done, f32[2,512,768]{2,1,0:T(8,128)S(1)} %copy-done.4), kind=kOutput, calls=%fused_computation.8 | convolution fusion | flops 3623878656 | bytes 5505024 | tf_op jit(solution)/shard_map/dot_general | solution.py:50
  169.0 2.0 pad_maximum_fusion
  171.1 0.0 reduce-scatter.5.cloned.1.call-update
  171.1 45.1 %reduce-scatter.5.cloned.1.call-done = f32[64,1536]{1,0:T(8,128)} async-done(((f32[512,1536]{1,0:T(8,128)}), f32[64,1536]{1,0:T(8,128)}) %reduce-scatter.5.cloned.1.call-update) | async-done | bytes 393232 | tf_op jit(solution)/shard_map/reduce_scatter | solution.py:57
  216.2 1.8 fusion.13
  (4 shorter events, 0.0 us)
Async XLA Ops:
  7.2 1.7 copy-start
  7.2 11.8 %copy-start.5 = (s32[12,125]{1,0:T(8,128)S(1)}, s32[12,125]{1,0:T(8,128)}, u32[]{:S(2)}) copy-start(s32[12,125]{1,0:T(8,128)} %param.9) | copy-start | bytes 18004
  7.2 12.0 %copy-start.8 = (s32[64]{0:T(128)S(1)}, s32[64]{0:T(128)}, u32[]{:S(2)}) copy-start(s32[64]{0:T(128)} %param.10) | copy-start | bytes 772
  7.2 49.9 %reduce-scatter.3.cloned.1.call-start = ((), (), s32[]{:S(2)}) async-start(), calls=%async_computation.2 | async-start | bytes 1966080 | tf_op jit(solution)/shard_map/reduce_scatter | solution.py:35
  18.9 45.9 %copy-start.3 = (f32[12,125,125]{2,1,0:T(8,128)S(1)}, f32[12,125,125]{2,1,0:T(8,128)}, u32[]{:S(2)}) copy-start(f32[12,125,125]{2,1,0:T(8,128)} %param.8) | copy-start | bytes 2250004
  18.9 140.5 %all-gather.2.cloned.1.call-start = ((), (), s32[]{:S(2)}) async-start(), calls=%async_computation.3 | async-start | bytes 3932160 | tf_op jit(solution)/shard_map/all_gather | solution.py:49
  19.2 0.6 copy-start.7
  57.1 9.1 %copy-start.1 = (f32[128,768]{1,0:T(8,128)S(1)}, f32[128,768]{1,0:T(8,128)}, u32[]{:S(2)}) copy-start(f32[128,768]{1,0:T(8,128)} %reduce-scatter.3.cloned.1.call-done) | copy-start | bytes 1179652
  62.7 3.5 %collective-permute-start = (f32[128,64]{1,0:T(8,128)}, f32[128,64]{1,0:T(8,128)}, u32[]{:S(2)}, u32[]{:S(2)}) collective-permute-start(f32[128,64]{1,0:T(8,128)} %bitcast.33), channel_id=1, source_target_pairs={{4,0},{8,4},{12,8},{16,12},{20,16},{24,20},{28,24},{5,1},{9,5},{13... | collective-permute-start | bytes 98312 | tf_op jit(solution)/shard_map/ppermute | solution.py:10
  72.8 19.0 %copy-start.2 = (f32[128,768]{1,0:T(8,128)S(1)}, f32[128,768]{1,0:T(8,128)}, u32[]{:S(2)}) copy-start(f32[128,768]{1,0:T(8,128)} %reduce-scatter.3.cloned.1.call-done) | copy-start | bytes 1179652
  72.8 19.0 %copy-start.6 = (f32[768]{0:T(1024)S(1)}, f32[768]{0:T(1024)}, u32[]{:S(2)}) copy-start(f32[768]{0:T(1024)} %param.11) | copy-start | bytes 9220
  87.7 5.2 %collective-permute-start.1 = (f32[128,64]{0,1:T(8,128)S(1)}, f32[128,64]{0,1:T(8,128)S(1)}, u32[]{:S(2)}, u32[]{:S(2)}) collective-permute-start(f32[128,64]{0,1:T(8,128)S(1)} %slice.29), channel_id=1, source_target_pairs={{0,4},{4,8},{8,12},{12,16},{16,20},{20,24},{24,28},{1,5},{5,9},{9,... | collective-permute-start | bytes 98312 | tf_op jit(solution)/shard_map/ppermute | solution.py:10
  95.2 120.9 %reduce-scatter.5.cloned.1.call-start = ((), (), s32[]{:S(2)}) async-start(), calls=%async_computation.4 | async-start | bytes 3538944 | tf_op jit(solution)/shard_map/reduce_scatter | solution.py:57
  159.4 5.6 %copy-start.4 = (f32[2,512,768]{2,1,0:T(8,128)S(1)}, f32[2,512,768]{2,1,0:T(8,128)}, u32[]{:S(2)}) copy-start(f32[2,512,768]{2,1,0:T(8,128)} %all-gather.2.cloned.1.call-done) | copy-start | bytes 9437188
Sparse Core Ops, SparseCore 0:
  19.0 37.9 reduce-scatter.2
  95.4 63.9 all-gather.1
  171.2 44.9 reduce-scatter.4
where the time goes:
time: 225 us; the launch traced here: 224 us
  waiting for transfers between devices  146 us (65%)
  matrix products  23.7 us (11%)
  local copies, waits for them, and re-layouts  19.3 us (9%)
  other arithmetic  15.2 us (7%)
  between operations  14 us (6%)
  starting transfers between devices  5.94 us (3%)
    all_gather x1, waiting for transfers between devices, local(): pieces = lax.all_gather(stacked, 'state', axis=1, tiled=True)  63.9 us
    reduce_scatter x1, waiting for transfers between devices, local(): lax.psum_scatter(partial_value, 'node', scatter_dimension=0, tiled=True)  45.1 us
    reduce_scatter x1, waiting for transfers between devices, local(): lax.psum_scatter(lax.dot_general(coeffs, states, (((0,), (1,)), ((), ()))...  37.2 us
    dot_general x1, matrix products, local(): lax.dot_general(coeffs, states, (((0,), (1,)), ((), ())), precision=lax.P...  10 us
    scatter-add x1, other arithmetic, apply_cells(): assembled = jnp.zeros(extended.shape, jnp.float32).at[:, connect.reshape(...  8.86 us
    ppermute x2, starting transfers between devices, shifted(): return lax.ppermute(shard, axis, pairs)  5.6 us
    dot_general x1, matrix products, local(): jnp.dot(pieces[1], states, precision=lax.Precision.HIGHEST, preferred_ele...  5.57 us
    gather x3, local copies, waits for them, and re-layouts, apply_cells(): cell_values = extended[:, connect]  5.51 us
  transfers between devices with their start and end apart: 5, of which 4 were waited for; matrix products, arithmetic and copies ran while one was open for 2% of the time, Pallas kernels for 0%

commit v1 on v0

v1 whole, which is shorter than its diff:
```python
import functools

import jax
import jax.numpy as jnp
from jax import lax
from jax.experimental import pallas as pl
from jax.experimental.pallas import tpu as pltpu
from jax.sharding import PartitionSpec as P

MESH = pl.DeviceIdType.MESH
NN = (((1,), (0,)), ((), ()))
NT = (((1,), (1,)), ((), ()))
BF = jnp.bfloat16
F32 = jnp.float32


def split(x):
    hi = x.astype(BF)
    return hi, (x - hi.astype(F32)).astype(BF)


def mul(a, b, dims):
    return lax.dot_general(a, b, dims, preferred_element_type=F32)


def mul3(a, b, dims):
    return mul(a[0], b[0], dims) + (mul(a[0], b[1], dims) + mul(a[1], b[0], dims))


def kernel(
    n_node, n_state,
    states, coeffs, cells, links, faces, mass,
    rot, hout, mout,
    ct, xhi, xlo, part, rrecv, lrecv, rout, lout,
    st, thi, tlo, ahi, alo, wbuf, whi, wlo, ghost, gsend, wghost,
    qbuf, qrecv,
    rs_send, rs_recv, ls_send, ls_recv, q_send, q_recv, g_sem, w_sem,
):
    me = lax.axis_index("node")
    pos = lax.axis_index("state")
    nodes = states.shape[0]
    width = states.shape[1]
    ext = st.shape[0]
    count = cells.shape[0]
    face = ext - nodes
    chunks = qbuf.shape[0]
    pieces = part.shape[0]
    rows = n_node * 8
    last = n_state - 1

    def peer(k):
        return lax.rem(me + k, n_node)

    barrier = pltpu.get_barrier_semaphore()
    for k in range(1, n_node):
        pl.semaphore_signal(barrier, inc=1, device_id={"node": peer(k)}, device_id_type=MESH)

    @pl.when(pos > 0)
    def _():
        pl.semaphore_signal(barrier, inc=1, device_id={"state": pos - 1}, device_id_type=MESH)

    @pl.when(pos < last)
    def _():
        pl.semaphore_signal(barrier, inc=1, device_id={"state": pos + 1}, device_id_type=MESH)

    hi, lo = split(states[...])
    xhi[pl.ds(0, nodes)] = hi
    xlo[pl.ds(0, nodes)] = lo
    ct[...] = coeffs[...].T.reshape(ct.shape)

    @pl.when(pos == 0)
    def _():
        rrecv[...] = jnp.zeros_like(rrecv)

    @pl.when(pos == last)
    def _():
        lrecv[...] = jnp.zeros_like(lrecv)

    face_t = (lax.broadcasted_iota(jnp.int32, (nodes, 128), 0) == faces[...]).astype(F32)
    face_rows = face_t.T.astype(BF)
    picked = mul(face_rows, hi, NN) + mul(face_rows, lo, NN)
    gsend[...] = picked[:face]

    def rotate(t):
        a = split(ct[:, t].reshape(rows, width))
        value = mul3(a, (xhi[pl.ds(0, nodes)], xlo[pl.ds(0, nodes)]), NT)
        part[pl.ds(2 * t, 2)] = value.reshape(2, rows // 2, nodes)

    rotate(0)
    @pl.when((pos > 0) & (pos < last))
    def _():
        pl.semaphore_wait(barrier, n_node + 1)

    @pl.when((pos == 0) | (pos == last))
    def _():
        pl.semaphore_wait(barrier, n_node)

    def ghost_copy(to):
        return pltpu.make_async_remote_copy(
            src_ref=gsend, dst_ref=ghost, send_sem=g_sem.at[0], recv_sem=g_sem.at[1],
            device_id={"node": to}, device_id_type=MESH,
        )

    def back_copy(to):
        return pltpu.make_async_remote_copy(
            src_ref=wbuf.at[pl.ds(nodes, face)], dst_ref=wghost, send_sem=w_sem.at[0], recv_sem=w_sem.at[1],
            device_id={"node": to}, device_id_type=MESH,
        )

    def right_copy(q):
        return pltpu.make_async_remote_copy(
            src_ref=rout.at[q], dst_ref=rrecv.at[q], send_sem=rs_send.at[q], recv_sem=rs_recv.at[q],
            device_id={"state": lax.rem(pos + 1, n_state)}, device_id_type=MESH,
        )

    def left_copy(q):
        return pltpu.make_async_remote_copy(
            src_ref=lout.at[q], dst_ref=lrecv.at[q], send_sem=ls_send.at[q], recv_sem=ls_recv.at[q],
            device_id={"state": lax.rem(pos + last, n_state)}, device_id_type=MESH,
        )

    def panel_copy(t, k):
        return pltpu.make_async_remote_copy(
            src_ref=qbuf.at[t, peer(k)], dst_ref=qrecv.at[t, k - 1],
            send_sem=q_send.at[t, k - 1], recv_sem=q_recv.at[t, k - 1],
            device_id={"node": peer(k)}, device_id_type=MESH,
        )

    def line_step(h):
        q = h - 2 * pos

        @pl.when((q >= 0) & (q < pieces))
        def _():
            @pl.when(pos > 0)
            def _():
                right_copy(q).wait_recv()

            @pl.when(pos < last)
            def _():
                rout[q] = part[q] + rrecv[q]
                right_copy(q).start()

        g = h - 2 * (last - pos)

        @pl.when((g >= 0) & (g < pieces))
        def _():
            @pl.when(pos < last)
            def _():
                left_copy(g).wait_recv()

            @pl.when(pos > 0)
            def _():
                lout[g] = part[g] + lrecv[g]
                left_copy(g).start()

    def panel(t):
        both = pl.ds(2 * t, 2)
        total = part[both] + rrecv[both] + lrecv[both]
        total = total.reshape(rows, nodes)
        tiles = total.reshape(n_node, 8, nodes)
        owned = rot.shape[0]
        mine = jnp.zeros((owned, 8, nodes), F32)
        for z in range(n_state):
            mine = jnp.where(pos == z, tiles[z * owned:(z + 1) * owned], mine)
        rot[:, t] = mine
        h = mul3(split(total), (whi[...], wlo[...]), NN)
        qbuf[t, :, :, pl.ds(0, width)] = h.reshape(n_node, 8, width)
        m = mul3(split(total * mass[...]), (xhi[pl.ds(0, nodes)], xlo[pl.ds(0, nodes)]), NN)
        qbuf[t, :, :, pl.ds(width, width)] = m.reshape(n_node, 8, width)
        for k in range(1, n_node):
            panel_copy(t, k).start()

    def finish(t):
        value = qbuf[t, me]
        for k in range(1, n_node):
            panel_copy(t, k).wait_recv()
            value = value + qrecv[t, k - 1]
        hout[t] = value[:, :width]
        mout[t] = value[:, width:]

    line_step(0)

    @pl.when(me > 0)
    def _():
        ghost_copy(lax.rem(me + n_node - 1, n_node)).start()

    if chunks > 1:
        rotate(1)
    line_step(1)

    st[...] = (
        lax.broadcasted_iota(jnp.int32, st.shape, 0) == links[...]
    ).astype(F32).astype(BF)

    for c in range(count):
        cell = cells[c]
        cell = 0.5 * (cell + cell.T)
        chi, clo = split(cell)
        pick = st[:, 128 * c:128 * (c + 1)]
        t_hi, t_lo = split(mul(chi, pick, NT) + mul(clo, pick, NT))
        thi[pl.ds(128 * c, 128)] = t_hi
        tlo[pl.ds(128 * c, 128)] = t_lo
    line_step(2)
    if chunks > 2:
        rotate(2)
    a_hi, a_lo = split(mul(st[...], thi[...], NN) + mul(st[...], tlo[...], NN))
    ahi[...] = a_hi
    alo[...] = a_lo
    line_step(3)

    @pl.when(me < n_node - 1)
    def _():
        ghost_copy(lax.rem(me + 1, n_node)).wait_recv()

    @pl.when(me == n_node - 1)
    def _():
        ghost[...] = jnp.zeros_like(ghost)

    g_hi, g_lo = split(ghost[...])
    xhi[pl.ds(nodes, face)] = g_hi
    xlo[pl.ds(nodes, face)] = g_lo
    wbuf[...] = mul3((ahi[...], alo[...]), (xhi[...], xlo[...]), NN)

    @pl.when(me < n_node - 1)
    def _():
        back_copy(lax.rem(me + 1, n_node)).start()

    line_step(4)
    if chunks > 3:
        rotate(3)
    line_step(5)

    @pl.when(me > 0)
    def _():
        back_copy(lax.rem(me + n_node - 1, n_node)).wait_recv()

    @pl.when(me == 0)
    def _():
        wghost[...] = jnp.zeros_like(wghost)

    b_hi, b_lo = split(wghost[...])
    face_cols = face_t[:, :face].astype(BF)
    w_hi, w_lo = split(wbuf[pl.ds(0, nodes)] + mul(face_cols, b_hi, NN) + mul(face_cols, b_lo, NN))
    whi[...] = w_hi
    wlo[...] = w_lo

    def body(u, carry):
        line_step(2 * u)

        @pl.when(u + 1 < chunks)
        def _():
            rotate(u + 1)

        line_step(2 * u + 1)
        t = u - last

        @pl.when(t >= 0)
        def _():
            panel(t)

        @pl.when(t >= 2)
        def _():
            finish(t - 2)

        return carry

    lax.fori_loop(3, chunks + last, body, 0)
    for t in range(max(chunks - 2, 0), chunks):
        finish(t)

    @pl.when(me > 0)
    def _():
        ghost_copy(lax.rem(me + n_node - 1, n_node)).wait_send()

    @pl.when(me < n_node - 1)
    def _():
        back_copy(lax.rem(me + 1, n_node)).wait_send()

    @pl.loop(0, pieces)
    def _(q):
        @pl.when(pos < last)
        def _():
            right_copy(q).wait_send()

        @pl.when(pos > 0)
        def _():
            left_copy(q).wait_send()

    @pl.loop(0, chunks)
    def _(t):
        for k in range(1, n_node):
            panel_copy(t, k).wait_send()


def local(n_node, n_state, states, coeffs, cell_matrix, connect, face_list, node_mass):
    nodes, width = states.shape
    block = coeffs.shape[1]
    count, npe = connect.shape
    face = face_list.shape[0]
    ext = nodes + face
    chunks = block // n_node // 8
    half = n_node * 4
    pieces = 2 * chunks
    owned = n_node // n_state
    cells = jnp.pad(cell_matrix, ((0, 0), (0, 128 - npe), (0, 128 - npe)))
    links = jnp.pad(connect, ((0, 0), (0, 128 - npe)), constant_values=-1).reshape(1, count * 128)
    faces = jnp.pad(face_list, (0, 128 - face), constant_values=-1).reshape(1, 128)
    vmem = pl.BlockSpec(memory_space=pltpu.VMEM)
    line = pltpu.VMEM((pieces, half, nodes), F32)
    rot, h, m = pl.pallas_call(
        functools.partial(kernel, n_node, n_state),
        out_shape=(
            jax.ShapeDtypeStruct((owned, chunks, 8, nodes), F32),
            jax.ShapeDtypeStruct((chunks, 8, width), F32),
            jax.ShapeDtypeStruct((chunks, 8, width), F32),
        ),
        in_specs=[vmem] * 6,
        out_specs=(vmem,) * 3,
        scratch_shapes=[
            pltpu.VMEM((n_node, chunks, 8, width), F32),
            pltpu.VMEM((ext, width), BF),
            pltpu.VMEM((ext, width), BF),
            line, line, line, line, line,
            pltpu.VMEM((ext, count * 128), BF),
            pltpu.VMEM((count * 128, ext), BF),
            pltpu.VMEM((count * 128, ext), BF),
            pltpu.VMEM((ext, ext), BF),
            pltpu.VMEM((ext, ext), BF),
            pltpu.VMEM((ext, width), F32),
            pltpu.VMEM((nodes, width), BF),
            pltpu.VMEM((nodes, width), BF),
            pltpu.VMEM((face, width), F32),
            pltpu.VMEM((face, width), F32),
            pltpu.VMEM((face, width), F32),
            pltpu.VMEM((chunks, n_node, 8, 2 * width), F32),
            pltpu.VMEM((chunks, n_node - 1, 8, 2 * width), F32),
            pltpu.SemaphoreType.DMA((pieces,)),
            pltpu.SemaphoreType.DMA((pieces,)),
            pltpu.SemaphoreType.DMA((pieces,)),
            pltpu.SemaphoreType.DMA((pieces,)),
            pltpu.SemaphoreType.DMA((chunks, n_node - 1)),
            pltpu.SemaphoreType.DMA((chunks, n_node - 1)),
            pltpu.SemaphoreType.DMA((2,)),
            pltpu.SemaphoreType.DMA((2,)),
        ],
        compiler_params=pltpu.CompilerParams(
            collective_id=0, has_side_effects=True, vmem_limit_bytes=60 * 1024 * 1024
        ),
    )(states, coeffs, cells, links, faces, node_mass.reshape(1, nodes))
    return rot.reshape(block // n_state, nodes), h.reshape(block // n_node, width), m.reshape(block // n_node, width)


def solution(mesh):
    return jax.shard_map(
        functools.partial(local, mesh.shape["node"], mesh.shape["state"]),
        mesh=mesh,
        in_specs=(
            P("node", "state"),
            P("state", None),
            P("node", None, None),
            P("node", None),
            P("node"),
            P("node"),
        ),
        out_specs=(P("state", "node"), P("node", "state"), P("node", "state")),
        check_vma=False,
    )
```

time: 225 us -> 82.8 us (0.37)
  waiting for transfers between devices: 146 us -> 0 us
  Pallas kernels: 0 us -> 71 us
  matrix products: 23.7 us -> 0 us
  other arithmetic: 15.2 us -> 0 us
  between operations: 14 us -> 0.64 us
  local copies, waits for them, and re-layouts: 19.3 us -> 10.8 us
  starting transfers between devices: 5.94 us -> 0 us
    reduce_scatter x2 -> x0, waiting for transfers between devices: 82.3 us -> none  [the longest x1 45.1 us: local(): lax.psum_scatter(partial_value, 'node', scatter_dimension=0, tiled=True)]
    pallas_call x0 -> x1, Pallas kernels: none -> 71 us  [local(): pl.pallas_call(functools.partial(kernel, n_node, n_state), out_shape=(jax...]
    all_gather x1 -> x0, waiting for transfers between devices: 63.9 us -> none  [local(): pieces = lax.all_gather(stacked, 'state', axis=1, tiled=True)]
    dot_general x4 -> x0, matrix products: 23.7 us -> none  [the longest x1 10 us: local(): lax.dot_general(coeffs, states, (((0,), (1,)), ((), ())), precision=lax.P...]
    scatter-add x2 -> x0, other arithmetic: 10.1 us -> none  [the longest x1 8.86 us: apply_cells(): assembled = jnp.zeros(extended.shape, jnp.float32).at[:, connect.reshape(...]
    gather x5 -> x0, local copies, waits for them, and re-layouts: 9.19 us -> none  [the longest x3 5.51 us: apply_cells(): cell_values = extended[:, connect]]
    ppermute x2 -> x0, starting transfers between devices: 5.6 us -> none  [shifted(): return lax.ppermute(shard, axis, pairs)]
    slice x3 -> x0, local copies, waits for them, and re-layouts: 3.57 us -> none  [the longest x1 1.79 us: local(): return (rotated, own_rows[:, :state_width], own_rows[:, state_width:])]
  transfers between devices with their start and end apart: 5 -> 0, of which waited for: 4 -> 0; matrix products, arithmetic and copies ran while one was open for 2% -> 0% of each run, Pallas kernels for 0% -> 0%
where the time goes in v1:
time: 82.8 us; the launch traced here: 82.5 us
  Pallas kernels  71 us (86%)
  local copies, waits for them, and re-layouts  10.8 us (13%)
    pallas_call x1, Pallas kernels, local(): pl.pallas_call(functools.partial(kernel, n_node, n_state), out_shape=(jax...  71 us
    unnamed x5, local copies, waits for them, and re-layouts  6.3 us
    pad x1, local copies, waits for them, and re-layouts, local(): cells = jnp.pad(cell_matrix, ((0, 0), (0, 128 - npe), (0, 128 - npe)))  2.09 us

profile of v1, /device:TPU:0, one launch (start us, length us, event | category | flops | bytes accessed | tf_op | source)
XLA Modules:
  0.0 82.5 jit_solution(7789075873731317881)
XLA Ops:
  0.6 1.2 %pad_bitcast_fusion.1.faces = s32[1,128]{1,0:T(1,128)} fusion(s32[64]{0:T(128)} %param.10), kind=kLoop, calls=%fused_computation.2 | loop fusion | bytes 768 | tf_op jit(solution)/shard_map/reshape | solution.py:307
  1.8 1.3 %reshape.26.mass = f32[1,768]{1,0:T(1,128)} reshape(f32[768]{0:T(1024)} %param.11) | data formatting | bytes 6144 | tf_op jit(solution)/shard_map/reshape | solution.py:349
  3.1 0.7 pad_bitcast_fusion
  3.8 0.6 copy.11
  4.4 2.1 %pad.12.cells = f32[12,128,128]{2,1,0:T(8,128)} pad(f32[12,125,125]{2,1,0:T(8,128)} %param.8, f32[]{:T(128)} %constant.1.clone.1), padding=0_0x0_3x0_3 | pad | bytes 1536436 | tf_op jit(solution)/shard_map/jit(_pad)/pad | solution.py:305
  6.5 71.0 %shard_map.85 = (f32[2,8,8,768]{3,2,1,0:T(8,128)}, f32[8,8,768]{2,1,0:T(8,128)}, f32[8,8,768]{2,1,0:T(8,128)}) custom-call(f32[768,768]{1,0:T(8,128)} %states.1, f32[768,512]{1,0:T(8,128)} %coeffs.1, f32[12,128,128]{2,1,0:T(8,128)} %pad.12.cells, s32[1,1536]{1,0:T(1,128)} %bitcast.14, s32[1,128]{1,0:T(1,128)} %pad_bitcast_fusion.1.faces, f32[1,768]{1,0:T(1,128)} %reshape.26.mass), custom_call_target="tpu_custom_call" | custom-call | tf_op jit(solution)/shard_map/pallas_call | solution.py:310
  77.5 1.8 %copy.15 = f32[128,768]{1,0:T(8,128)} copy(f32[128,768]{1,0:T(8,128)} %bitcast.11) | data formatting | bytes 786432
  79.3 1.6 %copy.16 = f32[64,768]{1,0:T(8,128)} copy(f32[64,768]{1,0:T(8,128)} %bitcast.13) | data formatting | bytes 393216
  80.9 1.6 %copy.17 = f32[64,768]{1,0:T(8,128)} copy(f32[64,768]{1,0:T(8,128)} %bitcast.12) | data formatting | bytes 393216

commit v2 on v1

v2 whole, which is shorter than its diff:
```python
import functools

import jax
import jax.numpy as jnp
from jax import lax
from jax.experimental import pallas as pl
from jax.experimental.pallas import tpu as pltpu
from jax.sharding import PartitionSpec as P

MESH = pl.DeviceIdType.MESH
NN = (((1,), (0,)), ((), ()))
NT = (((1,), (1,)), ((), ()))
BF = jnp.bfloat16
F32 = jnp.float32


def split(x):
    hi = x.astype(BF)
    return hi, (x - hi.astype(F32)).astype(BF)


def mul(a, b, dims):
    return lax.dot_general(a, b, dims, preferred_element_type=F32)


def mul3(a, b, dims):
    return mul(a[0], b[0], dims) + (mul(a[0], b[1], dims) + mul(a[1], b[0], dims))


def kernel(
    n_node, n_state,
    states, coeffs, cell_matrix, connect, face_list, node_mass,
    rot, hout, mout,
    ct, xhi, xlo, part, rrecv, lrecv, rout, lout,
    cells, links, st, thi, tlo, ahi, alo, wbuf, whi, wlo, ghost, gsend, wghost,
    tot, qbuf, pairs, qsum, qrecv,
    rs_send, rs_recv, ls_send, ls_recv, p_send, p_recv, q_send, q_recv, g_sem, w_sem,
):
    me = lax.axis_index("node")
    pos = lax.axis_index("state")
    core = lax.rem(me, 2)
    chip = lax.div(me, 2)
    partner = me + 1 - 2 * core
    nodes, width = states.shape
    ext = st.shape[0]
    count, npe = connect.shape
    face = ext - nodes
    chunks = qbuf.shape[0]
    pieces = part.shape[0]
    rows = n_node * 8
    chips = n_node // 2
    last = n_state - 1
    steps = pieces + 2 * last
    owned = rot.shape[0]
    x = (xhi.at[pl.ds(0, nodes)], xlo.at[pl.ds(0, nodes)])

    barrier = pltpu.get_barrier_semaphore()
    for k in range(1, n_node):
        pl.semaphore_signal(
            barrier, inc=1, device_id={"node": lax.rem(me + k, n_node)}, device_id_type=MESH
        )

    @pl.when(pos > 0)
    def _():
        pl.semaphore_signal(barrier, inc=1, device_id={"state": pos - 1}, device_id_type=MESH)

    @pl.when(pos < last)
    def _():
        pl.semaphore_signal(barrier, inc=1, device_id={"state": pos + 1}, device_id_type=MESH)

    hi, lo = split(states[...])
    x[0][...] = hi
    x[1][...] = lo
    ct[...] = coeffs[...].T.reshape(ct.shape)

    def rotate(first, number):
        rows_of = [ct[:, t].reshape(rows, width) for t in range(first, first + number)]
        a = split(rows_of[0] if number == 1 else jnp.concatenate(rows_of, 0))
        value = mul3(a, (x[0][...], x[1][...]), NT)
        part[pl.ds(4 * first, 4 * number)] = value.reshape(4 * number, rows // 4, nodes)

    rotate(0, 1)

    @pl.when(pos == 0)
    def _():
        rrecv[...] = jnp.zeros_like(rrecv)

    @pl.when(pos == last)
    def _():
        lrecv[...] = jnp.zeros_like(lrecv)

    @pl.when((pos > 0) & (pos < last))
    def _():
        pl.semaphore_wait(barrier, n_node + 1)

    @pl.when((pos == 0) | (pos == last))
    def _():
        pl.semaphore_wait(barrier, n_node)

    def ghost_copy(to):
        return pltpu.make_async_remote_copy(
            src_ref=gsend, dst_ref=ghost, send_sem=g_sem.at[0], recv_sem=g_sem.at[1],
            device_id={"node": to}, device_id_type=MESH,
        )

    def back_copy(to):
        return pltpu.make_async_remote_copy(
            src_ref=wbuf.at[pl.ds(nodes, face)], dst_ref=wghost, send_sem=w_sem.at[0], recv_sem=w_sem.at[1],
            device_id={"node": to}, device_id_type=MESH,
        )

    def right_copy(q):
        return pltpu.make_async_remote_copy(
            src_ref=rout.at[q], dst_ref=rrecv.at[q], send_sem=rs_send.at[q], recv_sem=rs_recv.at[q],
            device_id={"state": lax.rem(pos + 1, n_state)}, device_id_type=MESH,
        )

    def left_copy(q):
        return pltpu.make_async_remote_copy(
            src_ref=lout.at[q], dst_ref=lrecv.at[q], send_sem=ls_send.at[q], recv_sem=ls_recv.at[q],
            device_id={"state": lax.rem(pos + last, n_state)}, device_id_type=MESH,
        )

    def pair_copy(t):
        return pltpu.make_async_remote_copy(
            src_ref=qbuf.at[t, :, 1 - core], dst_ref=pairs.at[t],
            send_sem=p_send.at[t], recv_sem=p_recv.at[t],
            device_id={"node": partner}, device_id_type=MESH,
        )

    def panel_copy(t, k):
        to = lax.rem(chip + k, chips)
        return pltpu.make_async_remote_copy(
            src_ref=qsum.at[t, to], dst_ref=qrecv.at[t, k - 1],
            send_sem=q_send.at[t, k - 1], recv_sem=q_recv.at[t, k - 1],
            device_id={"node": 2 * to + core}, device_id_type=MESH,
        )

    def line_step(h):
        q = h - 2 * pos

        @pl.when((q >= 0) & (q < pieces))
        def _():
            @pl.when(pos > 0)
            def _():
                right_copy(q).wait_recv()

            @pl.when(pos < last)
            def _():
                rout[q] = part[q] + rrecv[q]
                right_copy(q).start()

        g = h - 2 * (last - pos)

        @pl.when((g >= 0) & (g < pieces))
        def _():
            @pl.when(pos < last)
            def _():
                left_copy(g).wait_recv()

            @pl.when(pos > 0)
            def _():
                lout[g] = part[g] + lrecv[g]
                left_copy(g).start()

    def line_steps(begin, end):
        @pl.loop(begin, end)
        def _(h):
            line_step(h)

    line_step(0)
    face_t = (
        lax.broadcasted_iota(jnp.int32, (nodes, face), 0) == face_list[...].reshape(1, face)
    ).astype(F32)
    face_cols = face_t.astype(BF)
    face_rows = face_t.T.astype(BF)
    gsend[...] = mul(face_rows, x[0][...], NN) + mul(face_rows, x[1][...], NN)

    @pl.when(me > 0)
    def _():
        ghost_copy(lax.rem(me + n_node - 1, n_node)).start()

    line_step(1)
    rotate(1, 1)
    line_step(2)
    cells[...] = jnp.zeros_like(cells)
    cells[:, :npe, :npe] = cell_matrix[...]
    links[...] = jnp.full(links.shape, -1, jnp.int32)
    links[:count, :npe] = connect[...]
    for c in range(count):
        st[:, 128 * c:128 * (c + 1)] = (
            lax.broadcasted_iota(jnp.int32, (ext, 128), 0) == links[c:c + 1]
        ).astype(F32).astype(BF)
    line_step(3)
    if chunks > 2:
        rotate(2, 2)
    line_step(4)
    for c in range(count):
        cell = cells[c]
        chi, clo = split(0.5 * (cell + cell.T))
        pick = st[:, 128 * c:128 * (c + 1)]
        t_hi, t_lo = split(mul(chi, pick, NT) + mul(clo, pick, NT))
        thi[pl.ds(128 * c, 128)] = t_hi
        tlo[pl.ds(128 * c, 128)] = t_lo
        if c % 3 == 2:
            line_step(5 + c // 3)
    done = 5 + count // 3
    quarter = ext // 4
    for r in range(4):
        picks = st[pl.ds(quarter * r, quarter)]
        a_hi, a_lo = split(mul(picks, thi[...], NN) + mul(picks, tlo[...], NN))
        ahi[pl.ds(quarter * r, quarter)] = a_hi
        alo[pl.ds(quarter * r, quarter)] = a_lo
        line_step(done)
        done += 1

    @pl.when(me < n_node - 1)
    def _():
        ghost_copy(lax.rem(me + 1, n_node)).wait_recv()

    @pl.when(me == n_node - 1)
    def _():
        ghost[...] = jnp.zeros_like(ghost)

    g_hi, g_lo = split(ghost[...])
    xhi[pl.ds(nodes, face)] = g_hi
    xlo[pl.ds(nodes, face)] = g_lo

    def apply(begin, size):
        at = pl.ds(begin, size)
        wbuf[at] = mul3((ahi[at], alo[at]), (xhi[...], xlo[...]), NN)

    apply(nodes, face)

    @pl.when(me < n_node - 1)
    def _():
        back_copy(lax.rem(me + 1, n_node)).start()

    line_step(done)
    done += 1
    for t in range(4, chunks, 2):
        rotate(t, 2)
        line_step(done)
        done += 1
    third = nodes // 3
    for r in range(3):
        apply(third * r, third)
        line_step(done)
        done += 1

    @pl.when(me > 0)
    def _():
        back_copy(lax.rem(me + n_node - 1, n_node)).wait_recv()

    @pl.when(me == 0)
    def _():
        wghost[...] = jnp.zeros_like(wghost)

    b_hi, b_lo = split(wghost[...])
    w_hi, w_lo = split(wbuf[pl.ds(0, nodes)] + mul(face_cols, b_hi, NN) + mul(face_cols, b_lo, NN))
    whi[...] = w_hi
    wlo[...] = w_lo
    line_step(done)
    done += 1

    def ready(t):
        return jnp.minimum(jnp.maximum(done + 2 * t, 4 * t + 4 + 2 * last), steps)

    def finish(t):
        value = qsum[t, chip]
        for k in range(1, chips):
            panel_copy(t, k).wait_recv()
            value = value + qrecv[t, k - 1]
        hout[t] = value[:, :width]
        mout[t] = value[:, width:]

    line_steps(done, ready(0))

    def body(t, carry):
        begin, end = ready(t), ready(t + 1)
        middle = jnp.minimum(begin + 1, end)
        every = pl.ds(4 * t, 4)
        total = (part[every] + rrecv[every] + lrecv[every]).reshape(rows, nodes)
        tot[...] = total.reshape(n_node, 8, nodes)
        rot[:, t] = tot[pl.ds(pos * owned, owned)]
        h = mul3(split(total), (whi[...], wlo[...]), NN)
        qbuf[t, :, :, :, pl.ds(0, width)] = h.reshape(chips, 2, 8, width)
        line_steps(begin, middle)
        total = tot[...].reshape(rows, nodes)
        m = mul3(split(total * node_mass[...].reshape(1, nodes)), (x[0][...], x[1][...]), NN)
        qbuf[t, :, :, :, pl.ds(width, width)] = m.reshape(chips, 2, 8, width)
        pair_copy(t).start()
        line_steps(middle, end)
        pair_copy(t).wait_recv()
        qsum[t] = qbuf[t, :, core] + pairs[t]
        for k in range(1, chips):
            panel_copy(t, k).start()

        @pl.when(t > 0)
        def _():
            finish(t - 1)

        return carry

    lax.fori_loop(0, chunks, body, 0)
    finish(chunks - 1)

    @pl.when(me > 0)
    def _():
        ghost_copy(lax.rem(me + n_node - 1, n_node)).wait_send()

    @pl.when(me < n_node - 1)
    def _():
        back_copy(lax.rem(me + 1, n_node)).wait_send()

    @pl.loop(0, pieces)
    def _(q):
        @pl.when(pos < last)
        def _():
            right_copy(q).wait_send()

        @pl.when(pos > 0)
        def _():
            left_copy(q).wait_send()

    @pl.loop(0, chunks)
    def _(t):
        pair_copy(t).wait_send()
        for k in range(1, chips):
            panel_copy(t, k).wait_send()


def deliver(a, b, c, a_out, b_out, c_out, sems):
    copies = [
        pltpu.make_async_copy(source, target, sems.at[i])
        for i, (source, target) in enumerate(((a, a_out), (b, b_out), (c, c_out)))
    ]
    for copy in copies:
        copy.start()
    for copy in copies:
        copy.wait()


def local(n_node, n_state, states, coeffs, cell_matrix, connect, face_list, node_mass):
    nodes, width = states.shape
    block = coeffs.shape[1]
    count = connect.shape[0]
    face = face_list.shape[0]
    ext = nodes + face
    chunks = block // n_node // 8
    pieces = 4 * chunks
    chips = n_node // 2
    owned = n_node // n_state
    vmem = pl.BlockSpec(memory_space=pltpu.VMEM)
    line = pltpu.VMEM((pieces, n_node * 2, nodes), F32)
    outs = pl.pallas_call(
        functools.partial(kernel, n_node, n_state),
        out_shape=(
            jax.ShapeDtypeStruct((owned, chunks, 8, nodes), F32),
            jax.ShapeDtypeStruct((chunks, 8, width), F32),
            jax.ShapeDtypeStruct((chunks, 8, width), F32),
        ),
        in_specs=[vmem] * 6,
        out_specs=(vmem,) * 3,
        scratch_shapes=[
            pltpu.VMEM((n_node, chunks, 8, width), F32),
            pltpu.VMEM((ext, width), BF),
            pltpu.VMEM((ext, width), BF),
            line, line, line, line, line,
            pltpu.VMEM((count, 128, 128), F32),
            pltpu.VMEM((-(-count // 8) * 8, 128), jnp.int32),
            pltpu.VMEM((ext, count * 128), BF),
            pltpu.VMEM((count * 128, ext), BF),
            pltpu.VMEM((count * 128, ext), BF),
            pltpu.VMEM((ext, ext), BF),
            pltpu.VMEM((ext, ext), BF),
            pltpu.VMEM((ext, width), F32),
            pltpu.VMEM((nodes, width), BF),
            pltpu.VMEM((nodes, width), BF),
            pltpu.VMEM((face, width), F32),
            pltpu.VMEM((face, width), F32),
            pltpu.VMEM((face, width), F32),
            pltpu.VMEM((n_node, 8, nodes), F32),
            pltpu.VMEM((chunks, chips, 2, 8, 2 * width), F32),
            pltpu.VMEM((chunks, chips, 8, 2 * width), F32),
            pltpu.VMEM((chunks, chips, 8, 2 * width), F32),
            pltpu.VMEM((chunks, chips - 1, 8, 2 * width), F32),
            pltpu.SemaphoreType.DMA((pieces,)),
            pltpu.SemaphoreType.DMA((pieces,)),
            pltpu.SemaphoreType.DMA((pieces,)),
            pltpu.SemaphoreType.DMA((pieces,)),
            pltpu.SemaphoreType.DMA((chunks,)),
            pltpu.SemaphoreType.DMA((chunks,)),
            pltpu.SemaphoreType.DMA((chunks, chips - 1)),
            pltpu.SemaphoreType.DMA((chunks, chips - 1)),
            pltpu.SemaphoreType.DMA((2,)),
            pltpu.SemaphoreType.DMA((2,)),
        ],
        compiler_params=pltpu.CompilerParams(
            collective_id=0, has_side_effects=True, vmem_limit_bytes=60 * 1024 * 1024
        ),
    )(states, coeffs, cell_matrix, connect, face_list, node_mass)
    shapes = ((block // n_state, nodes), (block // n_node, width), (block // n_node, width))
    anywhere = pl.BlockSpec(memory_space=pl.ANY)
    return pl.pallas_call(
        deliver,
        out_shape=tuple(jax.ShapeDtypeStruct(shape, F32) for shape in shapes),
        in_specs=[anywhere] * 3,
        out_specs=(anywhere,) * 3,
        scratch_shapes=[pltpu.SemaphoreType.DMA((3,))],
        compiler_params=pltpu.CompilerParams(vmem_limit_bytes=60 * 1024 * 1024),
    )(*(out.reshape(shape) for out, shape in zip(outs, shapes)))


def solution(mesh):
    return jax.shard_map(
        functools.partial(local, mesh.shape["node"], mesh.shape["state"]),
        mesh=mesh,
        in_specs=(
            P("node", "state"),
            P("state", None),
            P("node", None, None),
            P("node", None),
            P("node"),
            P("node"),
        ),
        out_specs=(P("state", "node"), P("node", "state"), P("node", "state")),
        check_vma=False,
    )
```

time: 82.8 us -> 107 us (1.29)
  Pallas kernels: 71 us -> 106 us
  local copies, waits for them, and re-layouts: 10.8 us -> 0 us
    pallas_call x0 -> x1, Pallas kernels: none -> 25 us  [local(): pl.pallas_call(deliver, out_shape=tuple((jax.ShapeDtypeStruct(shape, F32)...]
    pallas_call x1, Pallas kernels: 71 us -> 80.9 us  [local(): pl.pallas_call(functools.partial(kernel, n_node, n_state), out_shape=(jax...]
    unnamed x5 -> x0, local copies, waits for them, and re-layouts: 6.3 us -> none
    reshape x2 -> x0, local copies, waits for them, and re-layouts: 2.43 us -> none  [the longest x1 1.27 us: local(): node_mass.reshape(1, nodes)]
    pad x1 -> x0, local copies, waits for them, and re-layouts: 2.09 us -> none  [local(): cells = jnp.pad(cell_matrix, ((0, 0), (0, 128 - npe), (0, 128 - npe)))]
where the time goes in v2:
time: 107 us
  Pallas kernels  106 us (99%)
    pallas_call x1, Pallas kernels, local(): pl.pallas_call(functools.partial(kernel, n_node, n_state), out_shape=(jax...  80.9 us
    pallas_call x1, Pallas kernels, local(): pl.pallas_call(deliver, out_shape=tuple((jax.ShapeDtypeStruct(shape, F32)...  25 us

profile of v2, /device:TPU:0, one launch (start us, length us, event | category | flops | bytes accessed | tf_op | source)
XLA Modules:
  0.0 106.7 jit_solution(16019767879968792565)
XLA Ops:
  0.6 80.9 %shard_map.85 = (f32[2,8,8,768]{3,2,1,0:T(8,128)}, f32[8,8,768]{2,1,0:T(8,128)}, f32[8,8,768]{2,1,0:T(8,128)}) custom-call(f32[768,768]{1,0:T(8,128)} %states.1, f32[768,512]{1,0:T(8,128)} %coeffs.1, f32[12,125,125]{2,1,0:T(8,128)} %cell_matrix.1, s32[12,125]{1,0:T(8,128)} %connect.1, s32[64]{0:T(128)} %face_list.1, f32[768]{0:T(1024)} %node_mass.1), custom_call_target="tpu_custom_call" | custom-call | tf_op jit(solution)/shard_map/pallas_call | solution.py:356
  81.6 25.0 %shard_map.86 = (f32[128,768]{1,0:T(8,128)}, f32[64,768]{1,0:T(8,128)}, f32[64,768]{1,0:T(8,128)}) custom-call(f32[128,768]{1,0:T(8,128)} %bitcast.3, f32[64,768]{1,0:T(8,128)} %bitcast.4, f32[64,768]{1,0:T(8,128)} %bitcast.5), custom_call_target="tpu_custom_call" | custom-call | tf_op jit(solution)/shard_map/pallas_call | solution.py:405

commit v3 on v2

v3 whole, which is shorter than its diff:
```python
import functools

import jax
import jax.numpy as jnp
from jax import lax
from jax.experimental import pallas as pl
from jax.experimental.pallas import tpu as pltpu
from jax.sharding import PartitionSpec as P

MESH = pl.DeviceIdType.MESH
BF = jnp.bfloat16
F32 = jnp.float32


def split(x):
    hi = x.astype(BF)
    return hi, (x - hi.astype(F32)).astype(BF)


def mul(a, b):
    return jnp.dot(a, b, preferred_element_type=F32)


def mul3(a, b):
    return mul(a[0], b[0]) + (mul(a[0], b[1]) + mul(a[1], b[0]))


def mul3_stacked(a, b):
    rows = a.shape[0]
    hi, lo = split(a)
    both = mul(jnp.concatenate([hi, lo], 0), b[0])
    return both[:rows] + (both[rows:] + mul(hi, b[1]))


def kernel(
    n_node, n_state,
    states, coeffs, cell_matrix, connect, face_list, node_mass,
    rot, hout, mout,
    xhi, xlo, part, rrecv, lrecv, rout, lout,
    cells, links, st, twice, thi, tlo, ahi, alo, wbuf, whi, wlo, ghost, gsend, wghost,
    tot, qbuf, pairs, qsum, qrecv,
    rs_send, rs_recv, ls_send, ls_recv, p_send, p_recv, q_send, q_recv, g_sem, w_sem,
):
    me = lax.axis_index("node")
    pos = lax.axis_index("state")
    core = lax.rem(me, 2)
    chip = lax.div(me, 2)
    partner = me + 1 - 2 * core
    nodes, width = states.shape
    ext = st.shape[0]
    count, npe = connect.shape
    face = ext - nodes
    chunks, group, _ = hout.shape
    pieces = part.shape[0]
    per = pieces // chunks
    rows = n_node * group
    chips = n_node // 2
    last = n_state - 1
    steps = pieces + 2 * last
    owned = rot.shape[0]
    x = (xhi.at[pl.ds(0, nodes)], xlo.at[pl.ds(0, nodes)])

    barrier = pltpu.get_barrier_semaphore()
    for k in range(1, n_node):
        pl.semaphore_signal(
            barrier, inc=1, device_id={"node": lax.rem(me + k, n_node)}, device_id_type=MESH
        )

    @pl.when(pos > 0)
    def _():
        pl.semaphore_signal(barrier, inc=1, device_id={"state": pos - 1}, device_id_type=MESH)

    @pl.when(pos < last)
    def _():
        pl.semaphore_signal(barrier, inc=1, device_id={"state": pos + 1}, device_id_type=MESH)

    hi, lo = split(states[...])
    x[0][...] = hi
    x[1][...] = lo
    value = mul3((hi, lo), split(coeffs[...])).T
    value = value.reshape(n_node, chunks, group, nodes)
    owners = n_node // per
    for t in range(chunks):
        for j in range(per):
            part[per * t + j] = value[owners * j:owners * (j + 1), t].reshape(owners * group, nodes)

    @pl.when(pos == 0)
    def _():
        rrecv[...] = jnp.zeros_like(rrecv)

    @pl.when(pos == last)
    def _():
        lrecv[...] = jnp.zeros_like(lrecv)

    @pl.when((pos > 0) & (pos < last))
    def _():
        pl.semaphore_wait(barrier, n_node + 1)

    @pl.when((pos == 0) | (pos == last))
    def _():
        pl.semaphore_wait(barrier, n_node)

    def ghost_copy(to):
        return pltpu.make_async_remote_copy(
            src_ref=gsend, dst_ref=ghost, send_sem=g_sem.at[0], recv_sem=g_sem.at[1],
            device_id={"node": to}, device_id_type=MESH,
        )

    def back_copy(to):
        return pltpu.make_async_remote_copy(
            src_ref=wbuf.at[pl.ds(nodes, face)], dst_ref=wghost, send_sem=w_sem.at[0], recv_sem=w_sem.at[1],
            device_id={"node": to}, device_id_type=MESH,
        )

    def right_copy(q):
        return pltpu.make_async_remote_copy(
            src_ref=rout.at[q], dst_ref=rrecv.at[q], send_sem=rs_send.at[q], recv_sem=rs_recv.at[q],
            device_id={"state": lax.rem(pos + 1, n_state)}, device_id_type=MESH,
        )

    def left_copy(q):
        return pltpu.make_async_remote_copy(
            src_ref=lout.at[q], dst_ref=lrecv.at[q], send_sem=ls_send.at[q], recv_sem=ls_recv.at[q],
            device_id={"state": lax.rem(pos + last, n_state)}, device_id_type=MESH,
        )

    def pair_copy(e):
        return pltpu.make_async_remote_copy(
            src_ref=qbuf.at[e, :, 1 - core], dst_ref=pairs.at[e],
            send_sem=p_send.at[e], recv_sem=p_recv.at[e],
            device_id={"node": partner}, device_id_type=MESH,
        )

    def panel_copy(e, k):
        to = lax.rem(chip + k, chips)
        return pltpu.make_async_remote_copy(
            src_ref=qsum.at[e, to], dst_ref=qrecv.at[e, k - 1],
            send_sem=q_send.at[e, k - 1], recv_sem=q_recv.at[e, k - 1],
            device_id={"node": 2 * to + core}, device_id_type=MESH,
        )

    def line_step(h):
        q = h - 2 * pos

        @pl.when((q >= 0) & (q < pieces))
        def _():
            @pl.when(pos > 0)
            def _():
                right_copy(q).wait_recv()

            @pl.when(pos < last)
            def _():
                rout[q] = part[q] + rrecv[q]
                right_copy(q).start()

        g = h - 2 * (last - pos)

        @pl.when((g >= 0) & (g < pieces))
        def _():
            @pl.when(pos < last)
            def _():
                left_copy(g).wait_recv()

            @pl.when(pos > 0)
            def _():
                lout[g] = part[g] + lrecv[g]
                left_copy(g).start()

    def line_steps(begin, end):
        @pl.loop(begin, end)
        def _(h):
            line_step(h)

    line_step(0)
    face_t = (
        lax.broadcasted_iota(jnp.int32, (nodes, face), 0) == face_list[...].reshape(1, face)
    ).astype(F32)
    face_cols = face_t.astype(BF)
    face_rows = face_t.T.astype(BF)
    gsend[...] = mul(face_rows, x[0][...]) + mul(face_rows, x[1][...])

    @pl.when(me > 0)
    def _():
        ghost_copy(lax.rem(me + n_node - 1, n_node)).start()

    line_step(1)
    cells[...] = jnp.zeros_like(cells)
    cells[:, :npe, :npe] = cell_matrix[...]
    links[...] = jnp.full(links.shape, -1, jnp.int32)
    links[:count, :npe] = connect[...]
    columns = links[...].T
    done = 2
    for c in range(count):
        st[:, 128 * c:128 * (c + 1)] = (
            lax.broadcasted_iota(jnp.int32, (ext, 128), 0) == links[c:c + 1]
        ).astype(F32).astype(BF)
        pick = (
            lax.broadcasted_iota(jnp.int32, (128, ext), 1) == columns[:, c:c + 1]
        ).astype(F32).astype(BF)
        twice[pl.ds(0, 128)] = pick
        twice[pl.ds(128, 128)] = pick
        cell = cells[c]
        t_hi, t_lo = split(mul(jnp.concatenate(split(0.5 * (cell + cell.T)), 1), twice[...]))
        thi[pl.ds(128 * c, 128)] = t_hi
        tlo[pl.ds(128 * c, 128)] = t_lo
        if c % 4 == 3:
            line_step(done)
            done += 1
    for begin in range(0, ext - 128, 256):
        end = begin + 256 if ext - begin - 256 >= 128 else ext
        a_hi, a_lo = split(mul(st[...], thi[:, begin:end]) + mul(st[...], tlo[:, begin:end]))
        ahi[:, begin:end] = a_hi
        alo[:, begin:end] = a_lo
        line_step(done)
        done += 1

    @pl.when(me < n_node - 1)
    def _():
        ghost_copy(lax.rem(me + 1, n_node)).wait_recv()

    @pl.when(me == n_node - 1)
    def _():
        ghost[...] = jnp.zeros_like(ghost)

    g_hi, g_lo = split(ghost[...])
    xhi[pl.ds(nodes, face)] = g_hi
    xlo[pl.ds(nodes, face)] = g_lo

    at = pl.ds(nodes, face)
    wbuf[at] = mul3((ahi[at], alo[at]), (xhi[...], xlo[...]))

    @pl.when(me < n_node - 1)
    def _():
        back_copy(lax.rem(me + 1, n_node)).start()

    line_step(done)
    done += 1
    at = pl.ds(0, nodes)
    for begin in range(0, width, 256):
        cols = slice(begin, begin + 256)
        wbuf[at, cols] = mul3((ahi[at], alo[at]), (xhi[:, cols], xlo[:, cols]))
        line_step(done)
        done += 1

    @pl.when(me > 0)
    def _():
        back_copy(lax.rem(me + n_node - 1, n_node)).wait_recv()

    @pl.when(me == 0)
    def _():
        wghost[...] = jnp.zeros_like(wghost)

    b_hi, b_lo = split(wghost[...])
    w_hi, w_lo = split(wbuf[pl.ds(0, nodes)] + mul(face_cols, b_hi) + mul(face_cols, b_lo))
    whi[...] = w_hi
    wlo[...] = w_lo
    line_step(done)
    done += 1

    def ready(t):
        return jnp.minimum(jnp.maximum(done + 2 * t, per * (t + 1) + 2 * last), steps)

    def finish(t):
        for i, out in enumerate((hout, mout)):
            value = qsum[2 * t + i, chip]
            for k in range(1, chips):
                panel_copy(2 * t + i, k).wait_recv()
                value = value + qrecv[2 * t + i, k - 1]
            out[t] = value

    line_steps(done, ready(0))

    def body(t, carry):
        begin, end = ready(t), ready(t + 1)
        middle = jnp.minimum(begin + 1, end)
        every = pl.ds(per * t, per)
        total = (part[every] + rrecv[every] + lrecv[every]).reshape(rows, nodes)
        tot[...] = total.reshape(n_node, group, nodes)
        rot[:, t] = tot[pl.ds(pos * owned, owned)]
        qbuf[2 * t] = mul3_stacked(total, (whi[...], wlo[...])).reshape(chips, 2, group, width)
        pair_copy(2 * t).start()
        line_steps(begin, middle)
        total = tot[...].reshape(rows, nodes) * node_mass[...].reshape(1, nodes)
        qbuf[2 * t + 1] = mul3_stacked(total, (x[0][...], x[1][...])).reshape(chips, 2, group, width)
        pair_copy(2 * t + 1).start()
        for i in range(2):
            e = 2 * t + i
            pair_copy(e).wait_recv()
            qsum[e] = qbuf[e, :, core] + pairs[e]
            for k in range(1, chips):
                panel_copy(e, k).start()
            if i == 0:
                line_steps(middle, jnp.minimum(middle + 1, end))
        line_steps(jnp.minimum(middle + 1, end), end)

        @pl.when(t > 0)
        def _():
            finish(t - 1)

        return carry

    lax.fori_loop(0, chunks, body, 0)
    finish(chunks - 1)

    @pl.when(me > 0)
    def _():
        ghost_copy(lax.rem(me + n_node - 1, n_node)).wait_send()

    @pl.when(me < n_node - 1)
    def _():
        back_copy(lax.rem(me + 1, n_node)).wait_send()

    @pl.loop(0, pieces)
    def _(q):
        @pl.when(pos < last)
        def _():
            right_copy(q).wait_send()

        @pl.when(pos > 0)
        def _():
            left_copy(q).wait_send()

    @pl.loop(0, 2 * chunks)
    def _(e):
        pair_copy(e).wait_send()
        for k in range(1, chips):
            panel_copy(e, k).wait_send()


def deliver(a, b, c, a_out, b_out, c_out):
    a_out[...] = a[...]
    b_out[...] = b[...]
    c_out[...] = c[...]


def local(n_node, n_state, states, coeffs, cell_matrix, connect, face_list, node_mass):
    nodes, width = states.shape
    block = coeffs.shape[1]
    count = connect.shape[0]
    face = face_list.shape[0]
    ext = nodes + face
    group = 16
    chunks = block // n_node // group
    pieces = 4 * chunks
    chips = n_node // 2
    owned = n_node // n_state
    vmem = pl.BlockSpec(memory_space=pltpu.VMEM)
    line = pltpu.VMEM((pieces, n_node * group // 4, nodes), F32)
    outs = pl.pallas_call(
        functools.partial(kernel, n_node, n_state),
        out_shape=(
            jax.ShapeDtypeStruct((owned, chunks, group, nodes), F32),
            jax.ShapeDtypeStruct((chunks, group, width), F32),
            jax.ShapeDtypeStruct((chunks, group, width), F32),
        ),
        in_specs=[vmem] * 6,
        out_specs=(vmem,) * 3,
        scratch_shapes=[
            pltpu.VMEM((ext, width), BF),
            pltpu.VMEM((ext, width), BF),
            line, line, line, line, line,
            pltpu.VMEM((count, 128, 128), F32),
            pltpu.VMEM((-(-count // 8) * 8, 128), jnp.int32),
            pltpu.VMEM((ext, count * 128), BF),
            pltpu.VMEM((256, ext), BF),
            pltpu.VMEM((count * 128, ext), BF),
            pltpu.VMEM((count * 128, ext), BF),
            pltpu.VMEM((ext, ext), BF),
            pltpu.VMEM((ext, ext), BF),
            pltpu.VMEM((ext, width), F32),
            pltpu.VMEM((nodes, width), BF),
            pltpu.VMEM((nodes, width), BF),
            pltpu.VMEM((face, width), F32),
            pltpu.VMEM((face, width), F32),
            pltpu.VMEM((face, width), F32),
            pltpu.VMEM((n_node, group, nodes), F32),
            pltpu.VMEM((2 * chunks, chips, 2, group, width), F32),
            pltpu.VMEM((2 * chunks, chips, group, width), F32),
            pltpu.VMEM((2 * chunks, chips, group, width), F32),
            pltpu.VMEM((2 * chunks, chips - 1, group, width), F32),
            pltpu.SemaphoreType.DMA((pieces,)),
            pltpu.SemaphoreType.DMA((pieces,)),
            pltpu.SemaphoreType.DMA((pieces,)),
            pltpu.SemaphoreType.DMA((pieces,)),
            pltpu.SemaphoreType.DMA((2 * chunks,)),
            pltpu.SemaphoreType.DMA((2 * chunks,)),
            pltpu.SemaphoreType.DMA((2 * chunks, chips - 1)),
            pltpu.SemaphoreType.DMA((2 * chunks, chips - 1)),
            pltpu.SemaphoreType.DMA((2,)),
            pltpu.SemaphoreType.DMA((2,)),
        ],
        compiler_params=pltpu.CompilerParams(
            collective_id=0, has_side_effects=True, vmem_limit_bytes=60 * 1024 * 1024
        ),
    )(states, coeffs, cell_matrix, connect, face_list, node_mass)
    shapes = ((block // n_state, nodes), (block // n_node, width), (block // n_node, width))
    return pl.pallas_call(
        deliver,
        out_shape=tuple(jax.ShapeDtypeStruct(shape, F32) for shape in shapes),
        in_specs=[vmem] * 3,
        out_specs=(vmem,) * 3,
        compiler_params=pltpu.CompilerParams(vmem_limit_bytes=60 * 1024 * 1024),
    )(*(out.reshape(shape) for out, shape in zip(outs, shapes)))


def solution(mesh):
    return jax.shard_map(
        functools.partial(local, mesh.shape["node"], mesh.shape["state"]),
        mesh=mesh,
        in_specs=(
            P("node", "state"),
            P("state", None),
            P("node", None, None),
            P("node", None),
            P("node"),
            P("node"),
        ),
        out_specs=(P("state", "node"), P("node", "state"), P("node", "state")),
        check_vma=False,
    )
```

time: 107 us -> 69.1 us (0.65)
  Pallas kernels: 106 us -> 68.3 us
    pallas_call x1, Pallas kernels: 25 us -> 2.03 us  [local(): pl.pallas_call(deliver, out_shape=tuple((jax.ShapeDtypeStruct(shape, F32)...]
    pallas_call x1, Pallas kernels: 80.9 us -> 66.3 us  [local(): pl.pallas_call(functools.partial(kernel, n_node, n_state), out_shape=(jax...]
where the time goes in v3:
time: 69.1 us; the launch traced here: 68.9 us
  Pallas kernels  68.3 us (99%)
    pallas_call x1, Pallas kernels, local(): pl.pallas_call(functools.partial(kernel, n_node, n_state), out_shape=(jax...  66.3 us
    pallas_call x1, Pallas kernels, local(): pl.pallas_call(deliver, out_shape=tuple((jax.ShapeDtypeStruct(shape, F32)...  2.03 us

profile of v3, /device:TPU:0, one launch (start us, length us, event | category | flops | bytes accessed | tf_op | source)
XLA Modules:
  0.0 68.9 jit_solution(7947259280052514694)
XLA Ops:
  0.6 66.3 %shard_map.85 = (f32[2,4,16,768]{3,2,1,0:T(8,128)}, f32[4,16,768]{2,1,0:T(8,128)}, f32[4,16,768]{2,1,0:T(8,128)}) custom-call(f32[768,768]{1,0:T(8,128)} %states.1, f32[768,512]{1,0:T(8,128)} %coeffs.1, f32[12,125,125]{2,1,0:T(8,128)} %cell_matrix.1, s32[12,125]{1,0:T(8,128)} %connect.1, s32[64]{0:T(128)} %face_list.1, f32[768]{0:T(1024)} %node_mass.1), custom_call_target="tpu_custom_call" | custom-call | tf_op jit(solution)/shard_map/pallas_call | solution.py:349
  66.9 2.0 %shard_map.86 = (f32[128,768]{1,0:T(8,128)}, f32[64,768]{1,0:T(8,128)}, f32[64,768]{1,0:T(8,128)}) custom-call(f32[128,768]{1,0:T(8,128)} %bitcast.3, f32[64,768]{1,0:T(8,128)} %bitcast.4, f32[64,768]{1,0:T(8,128)} %bitcast.5), custom_call_target="tpu_custom_call" | custom-call | tf_op jit(solution)/shard_map/pallas_call | solution.py:397

commit v4 on v3

--- a/solution.py
+++ b/solution.py
@@ -172,6 +172,7 @@
             line_step(h)
 
     line_step(0)
+    line_step(1)
     face_t = (
         lax.broadcasted_iota(jnp.int32, (nodes, face), 0) == face_list[...].reshape(1, face)
     ).astype(F32)
@@ -183,13 +184,13 @@
     def _():
         ghost_copy(lax.rem(me + n_node - 1, n_node)).start()
 
-    line_step(1)
+    line_step(2)
     cells[...] = jnp.zeros_like(cells)
     cells[:, :npe, :npe] = cell_matrix[...]
     links[...] = jnp.full(links.shape, -1, jnp.int32)
     links[:count, :npe] = connect[...]
     columns = links[...].T
-    done = 2
+    done = 3
     for c in range(count):
         st[:, 128 * c:128 * (c + 1)] = (
             lax.broadcasted_iota(jnp.int32, (ext, 128), 0) == links[c:c + 1]
@@ -212,7 +213,8 @@
         ahi[:, begin:end] = a_hi
         alo[:, begin:end] = a_lo
         line_step(done)
-        done += 1
+        line_step(done + 1)
+        done += 2
 
     @pl.when(me < n_node - 1)
     def _():
@@ -240,7 +242,8 @@
         cols = slice(begin, begin + 256)
         wbuf[at, cols] = mul3((ahi[at], alo[at]), (xhi[:, cols], xlo[:, cols]))
         line_step(done)
-        done += 1
+        line_step(done + 1)
+        done += 2
 
     @pl.when(me > 0)
     def _():
@@ -267,6 +270,12 @@
                 panel_copy(2 * t + i, k).wait_recv()
                 value = value + qrecv[2 * t + i, k - 1]
             out[t] = value
+
+    def pass_on(e):
+        pair_copy(e).wait_recv()
+        qsum[e] = qbuf[e, :, core] + pairs[e]
+        for k in range(1, chips):
+            panel_copy(e, k).start()
 
     line_steps(done, ready(0))
 
@@ -279,27 +288,28 @@
         rot[:, t] = tot[pl.ds(pos * owned, owned)]
         qbuf[2 * t] = mul3_stacked(total, (whi[...], wlo[...])).reshape(chips, 2, group, width)
         pair_copy(2 * t).start()
+
+        @pl.when(t > 0)
+        def _():
+            pass_on(2 * t - 1)
+
         line_steps(begin, middle)
         total = tot[...].reshape(rows, nodes) * node_mass[...].reshape(1, nodes)
         qbuf[2 * t + 1] = mul3_stacked(total, (x[0][...], x[1][...])).reshape(chips, 2, group, width)
         pair_copy(2 * t + 1).start()
-        for i in range(2):
-            e = 2 * t + i
-            pair_copy(e).wait_recv()
-            qsum[e] = qbuf[e, :, core] + pairs[e]
-            for k in range(1, chips):
-                panel_copy(e, k).start()
-            if i == 0:
-                line_steps(middle, jnp.minimum(middle + 1, end))
-        line_steps(jnp.minimum(middle + 1, end), end)
-
-        @pl.when(t > 0)
-        def _():
-            finish(t - 1)
+        pass_on(2 * t)
+        line_steps(middle, end)
+
+        @pl.when(t > 1)
+        def _():
+            finish(t - 2)
 
         return carry
 
     lax.fori_loop(0, chunks, body, 0)
+    pass_on(2 * chunks - 1)
+    if chunks > 1:
+        finish(chunks - 2)
     finish(chunks - 1)
 
     @pl.when(me > 0)
@@ -339,7 +349,7 @@
     count = connect.shape[0]
     face = face_list.shape[0]
     ext = nodes + face
-    group = 16
+    group = 8
     chunks = block // n_node // group
     pieces = 4 * chunks
     chips = n_node // 2

time: 69.1 us -> 81.9 us (1.19)
  Pallas kernels: 68.3 us -> 81.1 us
    pallas_call x1, Pallas kernels: 66.3 us -> 79.1 us  [local(): pl.pallas_call(functools.partial(kernel, n_node, n_state), out_shape=(jax...]
where the time goes in v4:
time: 81.9 us; the launch traced here: 81.8 us
  Pallas kernels  81.1 us (99%)
    pallas_call x1, Pallas kernels, local(): pl.pallas_call(functools.partial(kernel, n_node, n_state), out_shape=(jax...  79.1 us
    pallas_call x1, Pallas kernels, local(): pl.pallas_call(deliver, out_shape=tuple((jax.ShapeDtypeStruct(shape, F32)...  2.03 us

profile of v4, /device:TPU:0, one launch (start us, length us, event | category | flops | bytes accessed | tf_op | source)
XLA Modules:
  0.0 81.8 jit_solution(13133567453298075814)
XLA Ops:
  0.6 79.1 %shard_map.85 = (f32[2,8,8,768]{3,2,1,0:T(8,128)}, f32[8,8,768]{2,1,0:T(8,128)}, f32[8,8,768]{2,1,0:T(8,128)}) custom-call(f32[768,768]{1,0:T(8,128)} %states.1, f32[768,512]{1,0:T(8,128)} %coeffs.1, f32[12,125,125]{2,1,0:T(8,128)} %cell_matrix.1, s32[12,125]{1,0:T(8,128)} %connect.1, s32[64]{0:T(128)} %face_list.1, f32[768]{0:T(1024)} %node_mass.1), custom_call_target="tpu_custom_call" | custom-call | tf_op jit(solution)/shard_map/pallas_call | solution.py:359
  79.7 2.0 %shard_map.86 = (f32[128,768]{1,0:T(8,128)}, f32[64,768]{1,0:T(8,128)}, f32[64,768]{1,0:T(8,128)}) custom-call(f32[128,768]{1,0:T(8,128)} %bitcast.3, f32[64,768]{1,0:T(8,128)} %bitcast.4, f32[64,768]{1,0:T(8,128)} %bitcast.5), custom_call_target="tpu_custom_call" | custom-call | tf_op jit(solution)/shard_map/pallas_call | solution.py:407

commit v5 on v4

--- a/solution.py
+++ b/solution.py
@@ -56,7 +56,8 @@
     rows = n_node * group
     chips = n_node // 2
     last = n_state - 1
-    steps = pieces + 2 * last
+    lag = 3
+    steps = pieces + lag * last
     owned = rot.shape[0]
     x = (xhi.at[pl.ds(0, nodes)], xlo.at[pl.ds(0, nodes)])
 
@@ -140,7 +141,7 @@
         )
 
     def line_step(h):
-        q = h - 2 * pos
+        q = h - lag * pos
 
         @pl.when((q >= 0) & (q < pieces))
         def _():
@@ -153,7 +154,7 @@
                 rout[q] = part[q] + rrecv[q]
                 right_copy(q).start()
 
-        g = h - 2 * (last - pos)
+        g = h - lag * (last - pos)
 
         @pl.when((g >= 0) & (g < pieces))
         def _():
@@ -171,8 +172,8 @@
         def _(h):
             line_step(h)
 
-    line_step(0)
-    line_step(1)
+    for done in range(lag):
+        line_step(done)
     face_t = (
         lax.broadcasted_iota(jnp.int32, (nodes, face), 0) == face_list[...].reshape(1, face)
     ).astype(F32)
@@ -184,13 +185,13 @@
     def _():
         ghost_copy(lax.rem(me + n_node - 1, n_node)).start()
 
-    line_step(2)
+    line_step(lag)
     cells[...] = jnp.zeros_like(cells)
     cells[:, :npe, :npe] = cell_matrix[...]
     links[...] = jnp.full(links.shape, -1, jnp.int32)
     links[:count, :npe] = connect[...]
     columns = links[...].T
-    done = 3
+    done = lag + 1
     for c in range(count):
         st[:, 128 * c:128 * (c + 1)] = (
             lax.broadcasted_iota(jnp.int32, (ext, 128), 0) == links[c:c + 1]
@@ -213,8 +214,7 @@
         ahi[:, begin:end] = a_hi
         alo[:, begin:end] = a_lo
         line_step(done)
-        line_step(done + 1)
-        done += 2
+        done += 1
 
     @pl.when(me < n_node - 1)
     def _():
@@ -242,8 +242,7 @@
         cols = slice(begin, begin + 256)
         wbuf[at, cols] = mul3((ahi[at], alo[at]), (xhi[:, cols], xlo[:, cols]))
         line_step(done)
-        line_step(done + 1)
-        done += 2
+        done += 1
 
     @pl.when(me > 0)
     def _():
@@ -261,7 +260,7 @@
     done += 1
 
     def ready(t):
-        return jnp.minimum(jnp.maximum(done + 2 * t, per * (t + 1) + 2 * last), steps)
+        return jnp.minimum(jnp.maximum(done + 2 * t, per * (t + 1) + lag * last), steps)
 
     def finish(t):
         for i, out in enumerate((hout, mout)):
@@ -349,7 +348,7 @@
     count = connect.shape[0]
     face = face_list.shape[0]
     ext = nodes + face
-    group = 8
+    group = 16
     chunks = block // n_node // group
     pieces = 4 * chunks
     chips = n_node // 2

time: 81.9 us -> 69 us (0.84)
  Pallas kernels: 81.1 us -> 68.2 us
    pallas_call x1, Pallas kernels: 79.1 us -> 66.2 us  [local(): pl.pallas_call(functools.partial(kernel, n_node, n_state), out_shape=(jax...]
where the time goes in v5:
time: 69 us; the launch traced here: 68.9 us
  Pallas kernels  68.2 us (99%)
    pallas_call x1, Pallas kernels, local(): pl.pallas_call(functools.partial(kernel, n_node, n_state), out_shape=(jax...  66.2 us
    pallas_call x1, Pallas kernels, local(): pl.pallas_call(deliver, out_shape=tuple((jax.ShapeDtypeStruct(shape, F32)...  2.03 us

profile of v5, /device:TPU:0, one launch (start us, length us, event | category | flops | bytes accessed | tf_op | source)
XLA Modules:
  0.0 68.9 jit_solution(4804071546073388081)
XLA Ops:
  0.6 66.2 %shard_map.85 = (f32[2,4,16,768]{3,2,1,0:T(8,128)}, f32[4,16,768]{2,1,0:T(8,128)}, f32[4,16,768]{2,1,0:T(8,128)}) custom-call(f32[768,768]{1,0:T(8,128)} %states.1, f32[768,512]{1,0:T(8,128)} %coeffs.1, f32[12,125,125]{2,1,0:T(8,128)} %cell_matrix.1, s32[12,125]{1,0:T(8,128)} %connect.1, s32[64]{0:T(128)} %face_list.1, f32[768]{0:T(1024)} %node_mass.1), custom_call_target="tpu_custom_call" | custom-call | tf_op jit(solution)/shard_map/pallas_call | solution.py:358
  66.8 2.0 %shard_map.86 = (f32[128,768]{1,0:T(8,128)}, f32[64,768]{1,0:T(8,128)}, f32[64,768]{1,0:T(8,128)}) custom-call(f32[128,768]{1,0:T(8,128)} %bitcast.3, f32[64,768]{1,0:T(8,128)} %bitcast.4, f32[64,768]{1,0:T(8,128)} %bitcast.5), custom_call_target="tpu_custom_call" | custom-call | tf_op jit(solution)/shard_map/pallas_call | solution.py:406

commit v6 on v5

--- a/solution.py
+++ b/solution.py
@@ -56,7 +56,7 @@
     rows = n_node * group
     chips = n_node // 2
     last = n_state - 1
-    lag = 3
+    lag = 2
     steps = pieces + lag * last
     owned = rot.shape[0]
     x = (xhi.at[pl.ds(0, nodes)], xlo.at[pl.ds(0, nodes)])
@@ -205,7 +205,7 @@
         t_hi, t_lo = split(mul(jnp.concatenate(split(0.5 * (cell + cell.T)), 1), twice[...]))
         thi[pl.ds(128 * c, 128)] = t_hi
         tlo[pl.ds(128 * c, 128)] = t_lo
-        if c % 4 == 3:
+        if c % 6 == 5:
             line_step(done)
             done += 1
     for begin in range(0, ext - 128, 256):
@@ -235,8 +235,6 @@
     def _():
         back_copy(lax.rem(me + 1, n_node)).start()
 
-    line_step(done)
-    done += 1
     at = pl.ds(0, nodes)
     for begin in range(0, width, 256):
         cols = slice(begin, begin + 256)
@@ -256,8 +254,6 @@
     w_hi, w_lo = split(wbuf[pl.ds(0, nodes)] + mul(face_cols, b_hi) + mul(face_cols, b_lo))
     whi[...] = w_hi
     wlo[...] = w_lo
-    line_step(done)
-    done += 1
 
     def ready(t):
         return jnp.minimum(jnp.maximum(done + 2 * t, per * (t + 1) + lag * last), steps)
@@ -350,11 +346,11 @@
     ext = nodes + face
     group = 16
     chunks = block // n_node // group
-    pieces = 4 * chunks
+    pieces = 2 * chunks
     chips = n_node // 2
     owned = n_node // n_state
     vmem = pl.BlockSpec(memory_space=pltpu.VMEM)
-    line = pltpu.VMEM((pieces, n_node * group // 4, nodes), F32)
+    line = pltpu.VMEM((pieces, n_node * group // 2, nodes), F32)
     outs = pl.pallas_call(
         functools.partial(kernel, n_node, n_state),
         out_shape=(

time: 69 us -> 76 us (1.10)
  Pallas kernels: 68.2 us -> 75.2 us
    pallas_call x1, Pallas kernels: 66.2 us -> 73.2 us  [local(): pl.pallas_call(functools.partial(kernel, n_node, n_state), out_shape=(jax...]
where the time goes in v6:
time: 76 us; the launch traced here: 75.9 us
  Pallas kernels  75.2 us (99%)
    pallas_call x1, Pallas kernels, local(): pl.pallas_call(functools.partial(kernel, n_node, n_state), out_shape=(jax...  73.2 us
    pallas_call x1, Pallas kernels, local(): pl.pallas_call(deliver, out_shape=tuple((jax.ShapeDtypeStruct(shape, F32)...  2.03 us

profile of v6, /device:TPU:0, one launch (start us, length us, event | category | flops | bytes accessed | tf_op | source)
XLA Modules:
  0.0 75.9 jit_solution(5982892543759094389)
XLA Ops:
  0.6 73.2 %shard_map.85 = (f32[2,4,16,768]{3,2,1,0:T(8,128)}, f32[4,16,768]{2,1,0:T(8,128)}, f32[4,16,768]{2,1,0:T(8,128)}) custom-call(f32[768,768]{1,0:T(8,128)} %states.1, f32[768,512]{1,0:T(8,128)} %coeffs.1, f32[12,125,125]{2,1,0:T(8,128)} %cell_matrix.1, s32[12,125]{1,0:T(8,128)} %connect.1, s32[64]{0:T(128)} %face_list.1, f32[768]{0:T(1024)} %node_mass.1), custom_call_target="tpu_custom_call" | custom-call | tf_op jit(solution)/shard_map/pallas_call | solution.py:354
  73.8 2.0 %shard_map.86 = (f32[128,768]{1,0:T(8,128)}, f32[64,768]{1,0:T(8,128)}, f32[64,768]{1,0:T(8,128)}) custom-call(f32[128,768]{1,0:T(8,128)} %bitcast.3, f32[64,768]{1,0:T(8,128)} %bitcast.4, f32[64,768]{1,0:T(8,128)} %bitcast.5), custom_call_target="tpu_custom_call" | custom-call | tf_op jit(solution)/shard_map/pallas_call | solution.py:402
